TPU v7x, 256 devices: a whole 4x4x8 slice. The times are simulated.
256 devices in a mesh: dp: 16 (over y_hi, z), blk: 16 (over y_lo, x, core).
Axes of the slice: x: 4, y: 4 (y_hi: 2, y_lo: 2; y = y_hi * 2 + y_lo), z: 8, core: 2. Of those that a mesh axis runs over, the one named last changes fastest.
Arguments:
- feats: bfloat16 [65536, 1536], P(('dp', 'blk')), may hold values from -1 to 1
- head_weight: bfloat16 [1536, 1536], replicated, may hold values from -1.5 to 1.5
- text_raw: bfloat16 [65536, 1536], P(('dp', 'blk')), may hold values from -1 to 1
- log_temp: float32 [1], replicated, may hold values from 2.4 to 2.8
- bias: float32 [1], replicated, may hold values from -2 to -1
Outputs:
- text_grad: float32 [65536, 1536], P(('dp', 'blk'))
- weight_grad: float32 [1536, 1536], P('dp', 'blk')
All inputs are finite; a program needn't handle non-finite values.
Results may differ from a plain program's by a relative error of at most 0.0016.
Values may be sent and summed in bfloat16 or wider, within the bound.
A program may use at most 128 MiB of HBM per device.

v0:
```python
import jax
import jax.numpy as jnp
from jax import lax
from jax.sharding import PartitionSpec as P

loss_scale = 4096.0


def unit_rows(x):
    inv = lax.rsqrt(jnp.sum(x * x, axis=-1, keepdims=True) + 1e-06)
    return (x * inv, inv)


def back_rows(grad, unit32, inv):
    return (grad - unit32 * jnp.sum(unit32 * grad, axis=-1, keepdims=True)) * inv


def local(feats, head_weight, text_raw, log_temp, bias):
    rows = feats.shape[0]
    scale = jnp.exp(log_temp[0])
    shift = bias[0]
    group = rows * lax.axis_size("blk")
    factor = loss_scale / (lax.axis_size("dp") * group)
    own_start = lax.axis_index("blk") * rows
    image_raw = jnp.dot(feats, head_weight, preferred_element_type=jnp.float32)
    img32, img_inv = unit_rows(image_raw)
    txt32, txt_inv = unit_rows(text_raw.astype(jnp.float32))
    image_unit = img32.astype(jnp.bfloat16)
    text_unit = txt32.astype(jnp.bfloat16)
    piece = lax.all_gather(text_unit, "blk", axis=0, tiled=True)
    logits = (
        scale
        * lax.dot_general(
            image_unit, piece, (((1,), (1,)), ((), ())), preferred_element_type=jnp.float32
        )
        + shift
    )
    left_ids = own_start + lax.broadcasted_iota(jnp.int32, logits.shape, 0)
    right_ids = lax.broadcasted_iota(jnp.int32, logits.shape, 1)
    diagonal = (left_ids == right_ids).astype(jnp.float32)
    coef = (factor * (jax.nn.sigmoid(logits) - diagonal)).astype(jnp.bfloat16)
    total = jnp.dot(coef, piece, preferred_element_type=jnp.float32)
    image_stored = coef
    image_side = scale * total
    image_grad = back_rows(image_side, img32, img_inv).astype(jnp.bfloat16)
    coef = image_stored
    text_sum = lax.psum_scatter(
        lax.dot_general(
            coef, image_unit, (((0,), (0,)), ((), ())), preferred_element_type=jnp.float32
        ),
        "blk",
        scatter_dimension=0,
        tiled=True,
    )
    text_grad = back_rows(scale * text_sum, txt32, txt_inv)
    partial_grad = lax.dot_general(
        feats, image_grad, (((0,), (0,)), ((), ())), preferred_element_type=jnp.float32
    )
    summed = lax.psum_scatter(partial_grad, "dp", scatter_dimension=0, tiled=True)
    weight_grad = lax.psum_scatter(summed, "blk", scatter_dimension=1, tiled=True)
    return (text_grad, weight_grad)


def solution(mesh):
    return jax.shard_map(
        local,
        mesh=mesh,
        in_specs=(P(("dp", "blk"), None), P(), P(("dp", "blk"), None), P(), P()),
        out_specs=(P(("dp", "blk"), None), P("dp", "blk")),
        check_vma=False,
    )
```

profile of v0, /device:TPU:1, one launch (start us, length us, event | category | flops | bytes accessed | tf_op | source)
XLA Modules:
  0.0 571.8 jit_solution(14383571778261092274)
XLA Ops:
  7.2 0.0 copy-start
  7.2 0.0 all-gather.2.cloned.1.call-start
  7.2 1.4 fusion.14
  8.7 2.2 fusion.10
  10.9 0.0 all-gather.2.cloned.1.call-update
  10.9 0.0 reduce-scatter.10.cloned.1.call-start
  12.3 0.0 copy-done
  12.3 3.8 multiply_reduce_fusion.1
  16.1 73.6 %all-gather.2.cloned.1.call-done = bf16[4096,1536]{1,0:T(8,128)(2,1)} async-done(((bf16[256,1536]{1,0:T(8,128)(2,1)}), bf16[4096,1536]{1,0:T(8,128)(2,1)}) %all-gather.2.cloned.1.call-update) | async-done | bytes 12582928 | tf_op jit(solution)/shard_map/all_gather | solution.py:30
  89.7 8.6 %fusion.7 = bf16[256,4096]{1,0:T(8,128)(2,1)S(1)} fusion(bf16[4096,1536]{1,0:T(8,128)(2,1)} %all-gather.2.cloned.1.call-done, s32[256]{0:T(256)S(1)} %iota_add_fusion, f32[]{:T(128)} %bitcast.12, f32[]{:T(128)} %bitcast, f32[256,1536]{1,0:T(8,128)S(1)} %get-tuple-element.7, f32[256]{0:T(256)S(1)} %add_rsqrt_fusion.1), kind=kOutput, calls=%fused_computation.9 | convolution fusion | flops 3232497664 | bytes 16254984 | tf_op jit(solution)/shard_map/dot_general | solution.py:33
  98.3 0.0 copy-start.4
  98.3 7.4 %multiply_reduce_fusion = (f32[256]{0:T(256)S(1)}, f32[256,1536]{1,0:T(8,128)S(1)}) fusion(f32[256,1536]{1,0:T(8,128)S(1)} %get-tuple-element.7, f32[256]{0:T(256)S(1)} %add_rsqrt_fusion.1, bf16[256,4096]{1,0:T(8,128)(2,1)S(1)} %fusion.7, bf16[4096,1536]{1,0:T(8,128)(2,1)} %all-gather.2.cloned.1.call-done, f32[]{:T(128)} %bitcast), kind=kOutput, calls=%fused_computation.22 | convolution fusion | flops 3222798080 | bytes 17827844 | tf_op jit(solution)/shard_map/dot_general | solution.py:42
  105.7 0.0 copy-done.4
  105.7 5.4 convolution_bitcast_fusion
  111.1 9.6 %copy.9 = f32[1536,1536]{1,0:T(8,128)} copy(f32[1536,1536]{0,1:T(8,128)} %convolution_bitcast_fusion) | data formatting | bytes 18874368
  120.8 0.0 reduce-scatter.10.cloned.1.call-update
  120.8 0.0 reduce-scatter.8.cloned.1.call-start
  120.9 228.7 %reduce-scatter.10.cloned.1.call-done = f32[96,1536]{1,0:T(8,128)} async-done(((f32[1536,1536]{1,0:T(8,128)}), f32[96,1536]{1,0:T(8,128)}) %reduce-scatter.10.cloned.1.call-update) | async-done | bytes 589840
  349.5 2.2 copy.10
  351.8 0.0 reduce-scatter.8.cloned.1.call-update
  351.8 0.0 reduce-scatter.6.cloned.1.call-start
  351.8 11.9 %fusion.17 = f32[4096,1536]{1,0:T(8,128)} fusion(bf16[256,4096]{1,0:T(8,128)(2,1)} %copy-done.4, f32[256,1536]{1,0:T(8,128)S(1)} %get-tuple-element.7, f32[256]{0:T(256)S(1)} %add_rsqrt_fusion.1), kind=kOutput, calls=%fused_computation.30 | convolution fusion | flops 3222011904 | bytes 28836864 | tf_op jit(solution)/shard_map/dot_general | solution.py:48
  363.8 0.0 copy-start.2
  363.8 0.0 reduce-scatter.6.cloned.1.call-update
  363.8 52.0 %reduce-scatter.8.cloned.1.call-done = f32[96,96]{0,1:T(8,128)} async-done(((f32[96,1536]{0,1:T(8,128)}), f32[96,96]{0,1:T(8,128)}) %reduce-scatter.8.cloned.1.call-update) | async-done | bytes 36880 | tf_op jit(solution)/shard_map/reduce_scatter | solution.py:60
  415.8 1.5 copy.8
  417.3 144.5 %reduce-scatter.6.cloned.1.call-done = f32[256,1536]{1,0:T(8,128)} async-done(((f32[4096,1536]{1,0:T(8,128)}), f32[256,1536]{1,0:T(8,128)}) %reduce-scatter.6.cloned.1.call-update) | async-done | bytes 1572880 | tf_op jit(solution)/shard_map/reduce_scatter | solution.py:47
  561.8 0.0 copy-done.2
  561.8 0.0 copy-start.3
  561.8 0.0 copy-start.1
  561.8 1.9 fusion.11
  563.7 0.0 copy-done.3
  563.7 1.5 fusion.13
  565.3 0.0 copy-done.1
  (3 shorter events, 0.0 us)
Async XLA Ops:
  7.2 5.1 copy-start
  7.2 82.5 %all-gather.2.cloned.1.call-start = ((), (), s32[]{:S(2)}) async-start(), calls=%async_computation.3 | async-start | bytes 13369344 | tf_op jit(solution)/shard_map/all_gather | solution.py:30
  10.9 338.6 %reduce-scatter.10.cloned.1.call-start = ((), (), s32[]{:S(2)}) async-start(), calls=%async_computation.6 | async-start | bytes 10027008
  98.3 7.4 %copy-start.4 = (bf16[256,4096]{1,0:T(8,128)(2,1)}, bf16[256,4096]{1,0:T(8,128)(2,1)S(1)}, u32[]{:S(2)}) copy-start(bf16[256,4096]{1,0:T(8,128)(2,1)S(1)} %fusion.7) | copy-start | bytes 6291460
  120.8 295.0 %reduce-scatter.8.cloned.1.call-start = ((), (), s32[]{:S(2)}) async-start(), calls=%async_computation.5 | async-start | bytes 835584 | tf_op jit(solution)/shard_map/reduce_scatter | solution.py:60
  351.8 210.0 %reduce-scatter.6.cloned.1.call-start = ((), (), s32[]{:S(2)}) async-start(), calls=%async_computation.4 | async-start | bytes 26738688 | tf_op jit(solution)/shard_map/reduce_scatter | solution.py:47
  363.8 198.0 %copy-start.2 = (bf16[256,1536]{1,0:T(8,128)(2,1)S(1)}, bf16[256,1536]{1,0:T(8,128)(2,1)}, u32[]{:S(2)}) copy-start(bf16[256,1536]{1,0:T(8,128)(2,1)} %param.7) | copy-start | bytes 2359300
  561.8 1.9 copy-start.3
  561.8 3.5 copy-start.1
Sparse Core Ops, SparseCore 0:
  11.0 78.6 all-gather.1
  120.9 228.5 reduce-scatter.9
  352.8 62.9 reduce-scatter.7
  418.2 143.5 reduce-scatter.5
where the time goes:
time: 573 us; the launch traced here: 572 us
  waiting for transfers between devices  499 us (87%)
  matrix products  37.1 us (6%)
  between operations  15.2 us (3%)
  local copies, waits for them, and re-layouts  13.4 us (2%)
  other arithmetic  7.13 us (1%)
    unnamed x5, waiting for transfers between devices  229 us
    reduce_scatter x1, waiting for transfers between devices, local(): lax.psum_scatter(lax.dot_general(coef, image_unit, (((0,), (0,)), ((), ()...  145 us
    all_gather x1, waiting for transfers between devices, local(): piece = lax.all_gather(text_unit, 'blk', axis=0, tiled=True)  73.6 us
    reduce_scatter x1, waiting for transfers between devices, local(): lax.psum_scatter(summed, 'blk', scatter_dimension=1, tiled=True)  52 us
    unnamed x13, local copies, waits for them, and re-layouts  13.4 us
    dot_general x1, matrix products, local(): lax.dot_general(coef, image_unit, (((0,), (0,)), ((), ())), preferred_ele...  11.9 us
  transfers between devices with their start and end apart: 4, of which 4 were waited for; matrix products, arithmetic and copies ran while one was open for 3% of the time, Pallas kernels for 0%

commit v1 on v0

v1 whole, which is shorter than its diff:
```python
import functools
import math

import jax
import jax.numpy as jnp
from jax import lax
from jax.experimental import pallas as pl
from jax.experimental.pallas import tpu as pltpu
from jax.sharding import PartitionSpec as P

MESH = pl.DeviceIdType.MESH
F32 = jnp.float32
BF16 = jnp.bfloat16
loss_scale = 4096.0

R = 256
E = 1536
F = 1536
H = 768
NX, NY, NZ = 4, 4, 8
OUT = 96

TEXT_CORE, TEXT_Y, TEXT_FWD = 0, 1, 2
XP1, XM1, XP2, XM2, XP3, XM3 = 3, 4, 5, 6, 7, 8
FT_CORE = 9
U_CORE = 13
CT_CORE = 17
G_CORE = 25
P_Y = 29
Z_RING = 33
Y_SUM = 57
X_SUM = 60
N_SEM = 64

P_CODE = 2.0**33
W_CODE = 2.0**4


def encode(v, s):
    v = v * s
    return (v * v * v).astype(BF16)


def decode(e, s):
    e = e.astype(F32)
    r = jnp.exp2(jnp.log2(jnp.maximum(jnp.abs(e), 1e-37)) * (1.0 / 3.0)) * (1.0 / s)
    return jnp.where(e > 0, r, jnp.where(e < 0, -r, 0.0))


def kernel(
    factor,
    lt_ref, bias_ref, feats_hbm, hw_hbm, text_hbm,
    tgrad_hbm, wgrad_ref,
    hw, ff, ft, u32, inv, uu, txr, tu, sw, ct, ctr, cfb, pp, yenc, yrecv,
    gall, ggr, zs, zr, zfin, zenc, yr2, ysum, xenc, xr3, scale_ref,
    load, ss, rs,
):
    dp, blk = lax.axis_index("dp"), lax.axis_index("blk")
    yh, z = dp // NZ, dp % NZ
    yl, x, c = blk // 8, (blk // 2) % NX, blk % 2
    y = yh * 2 + yl

    def dev(x, y, z, c):
        return ((y // 2) * NZ + z, (y % 2) * 8 + x * 2 + c)

    core = dev(x, y, z, 1 - c)
    xp, xm = dev((x + 1) % NX, y, z, c), dev((x + NX - 1) % NX, y, z, c)
    yp = dev(x, yh * 2 + 1 - yl, z, c)
    zp, zm = dev(x, y, (z + 1) % NZ, c), dev(x, y, (z + NZ - 1) % NZ, c)
    ys = [dev(x, (y + k) % NY, z, c) for k in (1, 2, 3)]
    xto = [(2 * c + k // 2, k % 2) for k in range(4)]
    xfrom = x // 2

    loads = [
        pltpu.make_async_copy(text_hbm, txr, load.at[0]),
        pltpu.make_async_copy(feats_hbm, ff.at[pl.ds(0, R)], load.at[1]),
        pltpu.make_async_copy(hw_hbm, hw, load.at[2]),
    ]
    for l in loads:
        l.start()
    bar = pltpu.get_barrier_semaphore()
    for d in [core, xp, xm, zp, zm] + ys:
        pl.semaphore_signal(bar, inc=1, device_id=d, device_id_type=MESH)
    for k in range(NX):
        @pl.when(jnp.logical_not((k == x) & (c == xfrom)))
        def _():
            pl.semaphore_signal(bar, inc=1, device_id=dev(k, y, z, xfrom), device_id_type=MESH)

    scale_ref[...] = jnp.exp(jnp.full((8, 128), lt_ref[0], F32))

    def scale():
        return scale_ref[0:1, 0:1]

    shift = bias_ref[0]

    def norm_text(i, _):
        rows = pl.ds(pl.multiple_of(i * 64, 64), 64)
        t = txr[rows, :].astype(F32)
        ti = lax.rsqrt(jnp.sum(t * t, axis=-1, keepdims=True) + 1e-06)
        tu[pl.ds(pl.multiple_of(c * R + i * 64, 64), 64), :] = (t * ti).astype(BF16)
        return 0

    loads[0].wait()
    lax.fori_loop(0, R // 64, norm_text, 0)

    pl.semaphore_wait(bar, 8 + 4 - jnp.where(c == xfrom, 1, 0))

    sent = []

    def send(src, dst, i, d, j=None):
        cp = pltpu.make_async_remote_copy(
            src, dst, ss.at[i], rs.at[i if j is None else j], device_id=d, device_id_type=MESH
        )
        cp.start()
        sent.append(cp)
        return cp

    trow = pl.ds(pl.multiple_of(c * R, R), R)
    tother = pl.ds(pl.multiple_of(2 * R + c * R, R), R)
    loads[1].wait()
    lo, hi = pl.ds(0, 128), pl.ds(128, 128)

    def half(b, k):
        return pl.ds(b * R + k * 128, 128)

    xp1 = send(ff.at[lo], ff.at[half(1, 0)], XP1, xp)
    xm1 = send(ff.at[hi], ff.at[half(1, 1)], XM1, xm)
    t_y = send(tu.at[trow], tu.at[tother], TEXT_Y, yp)
    t_core = send(tu.at[trow], tu.at[trow], TEXT_CORE, core)
    xp2 = send(ff.at[hi], ff.at[half(2, 0)], XP2, xp)
    xm2 = send(ff.at[lo], ff.at[half(2, 1)], XM2, xm)
    loads[2].wait()

    def rows_of(b, n=R):
        return pl.ds(pl.multiple_of(b * R, R), n)

    ft_cp, u_cp, ct_cp, g_cp = {}, {}, {}, {}

    def unit(b):
        rows = pl.ds(b * R, R)

        def raw(n, _):
            cols = pl.ds(pl.multiple_of(n * 256, 256), 256)
            u32[rows, cols] = jnp.dot(ff[rows, :], hw[:, cols], preferred_element_type=F32)
            return 0

        lax.fori_loop(0, 6, raw, 0)

        def norm(i, _):
            r = pl.ds(pl.multiple_of(b * R + i * 64, 64), 64)
            v = u32[r, :]
            iv = lax.rsqrt(jnp.sum(v * v, axis=-1, keepdims=True) + 1e-06)
            v = v * iv
            inv[r, :] = iv
            u32[r, :] = v
            uu[pl.ds(pl.multiple_of(b * R + i * 64, 64), 64), :] = v.astype(BF16)
            return 0

        lax.fori_loop(0, 4, norm, 0)
        u_cp[b] = send(uu.at[rows], uu.at[pl.ds(4 * R + b * R, R)], U_CORE + b, core)

    def transpose(b):
        rows = pl.ds(b * R, R)

        def tr(n, _):
            cols = pl.ds(pl.multiple_of(n * 256, 256), 256)
            ft[cols, pl.ds(b * R, R)] = ff[rows, cols].T
            return 0

        lax.fori_loop(0, 6, tr, 0)
        ft_cp[b] = send(
            ft.at[:, pl.ds(b * R, R)], ft.at[:, pl.ds(4 * R + b * R, R)], FT_CORE + b, core
        )

    def piece(b, h):
        rows = rows_of(b)
        for k in range(2):
            trows = pl.ds((2 * h + k) * R, R)
            logits = lax.dot_general(
                uu[rows, :], tu[trows, :], (((1,), (1,)), ((), ())), preferred_element_type=F32
            )
            logits = scale() * logits + shift
            p = jax.nn.sigmoid(logits)
            if h == 0 and isinstance(b, int) and b == 0:
                i = lax.broadcasted_iota(jnp.int32, p.shape, 0)
                j = lax.broadcasted_iota(jnp.int32, p.shape, 1)
                p = p - jnp.where((i == j) & (c == k), 1.0, 0.0)
            cf = (factor * p).astype(BF16)
            cfb[:, pl.ds(k * R, R)] = cf
            ct[b, h, k] = cf.T

    def exchange(b, h):
        ct_cp[b, h] = send(ct.at[b, h, 1 - c], ctr.at[b, h], CT_CORE + 2 * b + h, core)

    def side(b, h, first):
        rows2 = pl.ds(2 * h * R, 2 * R)

        def tile(n, _):
            cols = pl.ds(pl.multiple_of(n * 256, 256), 256)
            r = pl.ds(pl.multiple_of((n // 3) * 1024 + b * R, R), R)
            cc = pl.ds(pl.multiple_of((n % 3) * 256, 256), 256)
            v = jnp.dot(cfb[...], tu[rows2, cols], preferred_element_type=F32)
            sw[r, cc] = v if first else sw[r, cc] + v
            return 0

        lax.fori_loop(0, 6, tile, 0)

    def text_side(b, h, first):
        def tile(n, _):
            cols = pl.ds(pl.multiple_of(n * 256, 256), 256)
            v = jnp.dot(ct[b, h, c], uu[pl.ds(b * R, R), cols], preferred_element_type=F32)
            v = v + jnp.dot(ctr[b, h], uu[pl.ds(4 * R + b * R, R), cols], preferred_element_type=F32)
            pp[h, :, cols] = v if first else pp[h, :, cols] + v
            return 0

        lax.fori_loop(0, 6, tile, 0)

    unit(0)
    t_core.wait_recv()
    piece(0, 0)
    exchange(0, 0)
    side(0, 0, True)
    transpose(0)
    xp1.wait_recv()
    xp3 = send(ff.at[half(1, 0)], ff.at[half(3, 0)], XP3, xp)
    xm1.wait_recv()
    xm3 = send(ff.at[half(1, 1)], ff.at[half(3, 1)], XM3, xm)
    unit(1)
    piece(1, 0)
    exchange(1, 0)
    side(1, 0, True)
    u_cp[0].wait_recv()
    ct_cp[0, 0].wait_recv()
    text_side(0, 0, True)
    transpose(1)
    t_y.wait_recv()
    t_fwd = send(tu.at[tother], tu.at[tother], TEXT_FWD, core)
    xp2.wait_recv()
    xm2.wait_recv()
    unit(2)
    u_cp[1].wait_recv()
    ct_cp[1, 0].wait_recv()
    text_side(1, 0, False)
    piece(2, 0)
    exchange(2, 0)
    side(2, 0, True)
    t_fwd.wait_recv()
    for b in range(3):
        piece(b, 1)
        exchange(b, 1)
        side(b, 1, False)
        if b == 0:
            u_cp[2].wait_recv()
            ct_cp[2, 0].wait_recv()
            text_side(2, 0, False)
        else:
            ct_cp[b - 1, 1].wait_recv()
            text_side(b - 1, 1, b == 1)
    transpose(2)
    xp3.wait_recv()
    xm3.wait_recv()
    unit(3)
    piece(3, 1)
    exchange(3, 1)
    ct_cp[2, 1].wait_recv()
    text_side(2, 1, False)
    u_cp[3].wait_recv()
    ct_cp[3, 1].wait_recv()
    text_side(3, 1, False)
    p_cp = []
    for i in range(4):
        r = pl.ds(i * 64, 64)
        yenc[r, :] = encode(pp[1, r, :], P_CODE)
        p_cp.append(send(yenc.at[r], yrecv.at[r], P_Y + i, yp))
    side(3, 1, True)
    piece(3, 0)
    exchange(3, 0)
    side(3, 0, False)
    transpose(3)

    def image_grad(b):
        def chunk(i, _):
            r0 = b * R + i * 64
            r = pl.ds(pl.multiple_of(r0, 64), 64)
            rl = pl.ds(pl.multiple_of(1024 + r0, 64), 64)
            s = scale()
            g0, g1 = s * sw[r, :], s * sw[rl, :]
            v0, v1 = u32[r, pl.ds(0, H)], u32[r, pl.ds(H, H)]
            d = jnp.sum(v0 * g0, axis=-1, keepdims=True) + jnp.sum(v1 * g1, axis=-1, keepdims=True)
            iv = inv[r, :]
            g0 = ((g0 - v0 * d) * iv).astype(BF16)
            g1 = ((g1 - v1 * d) * iv).astype(BF16)
            for k in range(2):
                gall[k, r, pl.ds(0, 384)] = g0[:, k * 384 : k * 384 + 384]
                gall[k, r, pl.ds(384, 384)] = g1[:, k * 384 : k * 384 + 384]
            return 0

        lax.fori_loop(0, 4, chunk, 0)
        rows = pl.ds(b * R, R)
        g_cp[b] = send(gall.at[1 - c, rows], ggr.at[rows], G_CORE + b, core)

    for b in range(4):
        image_grad(b)
    ct_cp[3, 0].wait_recv()
    text_side(3, 0, False)
    for b in range(4):
        ft_cp[b].wait_recv()
        g_cp[b].wait_recv()

    def weight(n):
        cols = pl.ds(n * 256, 256)

        def tile(m, _):
            r = pl.ds(pl.multiple_of(m * 256, 256), 256)
            v = jnp.dot(ft[r, pl.ds(0, 1024)], gall[c, :, cols], preferred_element_type=F32)
            sw[r, cols] = v + jnp.dot(ft[r, pl.ds(1024, 1024)], ggr[:, cols], preferred_element_type=F32)
            return 0

        lax.fori_loop(0, 6, tile, 0)

    def own(n, zz, k):
        return sw[pl.ds(pl.multiple_of(k * H + zz * OUT, 32), OUT), pl.ds(n * 256, 256)]

    ring = {}

    def step(n, s):
        cps = []
        for d in range(2):
            zz = (z + (4 - s if d == 0 else NZ - 4 + s)) % NZ
            i = (n * 2 + d) * 4 + s
            if s:
                ring[n, s - 1][d].wait_recv()
            for k in range(2):
                if s == 0 and k != d:
                    continue
                v = own(n, zz, k)
                if s > 1 or (s == 1 and k == d):
                    v = v + decode(zr[i - 1, pl.ds(k * OUT, OUT), :], W_CODE)
                zs[i, pl.ds(k * OUT, OUT), :] = encode(v, W_CODE)
            r = pl.ds(d * OUT, OUT) if s == 0 else pl.ds(0, 2 * OUT)
            cps.append(send(zs.at[i, r], zr.at[i, r], Z_RING + i, zp if d == 0 else zm))
        ring[n, s] = cps

    def final(n):
        for d in range(2):
            ring[n, 3][d].wait_recv()
        for k in range(2):
            r = pl.ds(k * OUT, OUT)
            v = own(n, z, k)
            for d in range(2):
                v = v + decode(zr[(n * 2 + d) * 4 + 3, r, :], W_CODE)
            zfin[r, pl.ds(n * 256, 256)] = v
            zenc[r, pl.ds(n * 256, 256)] = encode(v, W_CODE)

    out_cp = []

    def text_out(i):
        p_cp[i].wait_recv()
        r = pl.ds(i * 64, 64)
        t = txr[r, :].astype(F32)
        ti = lax.rsqrt(jnp.sum(t * t, axis=-1, keepdims=True) + 1e-06)
        t = t * ti
        g = scale() * (pp[0, r, :] + decode(yrecv[r, :], P_CODE))
        pp[0, r, :] = (g - t * jnp.sum(t * g, axis=-1, keepdims=True)) * ti
        cp = pltpu.make_async_copy(pp.at[0, r], tgrad_hbm.at[r], load.at[3 + i])
        cp.start()
        out_cp.append(cp)

    weight(0)
    step(0, 0)
    weight(1)
    step(1, 0)
    step(0, 1)
    weight(2)
    step(2, 0)
    step(1, 1)
    step(0, 2)
    text_out(0)
    step(2, 1)
    text_out(1)
    step(1, 2)
    step(0, 3)
    text_out(2)
    step(2, 2)
    text_out(3)
    step(1, 3)
    final(0)
    step(2, 3)
    final(1)
    final(2)

    def zslice(yy):
        return (
            pl.ds(pl.multiple_of((yy // 2) * OUT, 32), OUT),
            pl.ds(pl.multiple_of((yy % 2) * 384, 128), 384),
        )

    y_cp = []
    for k in range(3):
        r, cc = zslice((y + k + 1) % NY)
        y_cp.append(send(zenc.at[r, cc], yr2.at[k], Y_SUM + k, ys[k]))
    r, cc = zslice(y)
    v = zfin[r, cc]
    for k in range(3):
        y_cp[k].wait_recv()
        v = v + decode(yr2[k], W_CODE)
    ysum[...] = v
    xenc[...] = encode(v, W_CODE)

    cps = []
    for k in range(4):
        xx, kc = xto[k]
        cols = pl.ds(128 * (k // 2), 256)
        cp = pltpu.make_async_remote_copy(
            xenc.at[:, cols], xr3.at[x], ss.at[X_SUM + k], rs.at[X_SUM + x],
            device_id=dev(xx, y, z, kc), device_id_type=MESH,
        )
        mine = (xx == x) & (kc == c)

        @pl.when(jnp.logical_not(mine))
        def _():
            cp.start()

        @pl.when(mine)
        def _():
            xr3[x] = xenc[:, cols]

        cps.append((cp, mine))
    for k in range(4):
        @pl.when(jnp.logical_not((k == x) & (c == xfrom)))
        def _():
            pltpu.make_async_remote_copy(
                xenc.at[:, pl.ds(0, 256)], xr3.at[k], ss.at[X_SUM + k], rs.at[X_SUM + k],
                device_id=core, device_id_type=MESH,
            ).wait_recv()

    v = decode(xr3[0], W_CODE)
    for k in range(1, 4):
        v = v + decode(xr3[k], W_CODE)
    mine = 2 * (x % 2) + c
    out = v[:, :OUT]
    for k, off in ((1, 96), (2, 64), (3, 160)):
        out = jnp.where(mine == k, pltpu.roll(v, 256 - off, 1)[:, :OUT], out)
    wgrad_ref[...] = out

    for cp in sent:
        cp.wait_send()
    for cp, mine in cps:
        @pl.when(jnp.logical_not(mine))
        def _():
            cp.wait_send()
    for cp in out_cp:
        cp.wait()


def local(feats, head_weight, text_raw, log_temp, bias):
    rows = feats.shape[0]
    factor = loss_scale / (lax.axis_size("dp") * rows * lax.axis_size("blk"))
    vmem = pltpu.VMEM
    scratch = [
        vmem((F, E), BF16),
        vmem((4 * R, F), BF16),
        vmem((F, 8 * R), BF16),
        vmem((4 * R, E), F32),
        vmem((4 * R, 1), F32),
        vmem((8 * R, E), BF16),
        vmem((R, E), BF16),
        vmem((4 * R, E), BF16),
        vmem((8 * R, H), F32),
        vmem((4, 2, 2, R, R), BF16),
        vmem((4, 2, R, R), BF16),
        vmem((R, 2 * R), BF16),
        vmem((2, R, E), F32),
        vmem((R, E), BF16),
        vmem((R, E), BF16),
        vmem((2, 4 * R, H), BF16),
        vmem((4 * R, H), BF16),
        vmem((24, 2 * OUT, 256), BF16),
        vmem((24, 2 * OUT, 256), BF16),
        vmem((2 * OUT, H), F32),
        vmem((2 * OUT, H), BF16),
        vmem((3, OUT, 384), BF16),
        vmem((OUT, 384), F32),
        vmem((OUT, 384), BF16),
        vmem((4, OUT, 256), BF16),
        vmem((8, 128), F32),
        pltpu.SemaphoreType.DMA((7,)),
        pltpu.SemaphoreType.DMA((N_SEM,)),
        pltpu.SemaphoreType.DMA((N_SEM,)),
    ]
    anyspec = pl.BlockSpec(memory_space=pl.ANY)
    smem = pl.BlockSpec(memory_space=pltpu.SMEM)
    return pl.pallas_call(
        functools.partial(kernel, factor),
        out_shape=(
            jax.ShapeDtypeStruct((R, E), F32),
            jax.ShapeDtypeStruct((OUT, OUT), F32),
        ),
        in_specs=[smem, smem, anyspec, anyspec, anyspec],
        out_specs=(anyspec, pl.BlockSpec(memory_space=pltpu.VMEM)),
        scratch_shapes=scratch,
        compiler_params=pltpu.CompilerParams(
            collective_id=0, has_side_effects=True, vmem_limit_bytes=63 * 1024 * 1024
        ),
        cost_estimate=pl.CostEstimate(
            flops=20_000_000_000, bytes_accessed=8_000_000, transcendentals=4_000_000
        ),
    )(log_temp, bias, feats, head_weight, text_raw)


def solution(mesh):
    return jax.shard_map(
        local,
        mesh=mesh,
        in_specs=(P(("dp", "blk"), None), P(), P(("dp", "blk"), None), P(), P()),
        out_specs=(P(("dp", "blk"), None), P("dp", "blk")),
        check_vma=False,
    )
```

time: 573 us -> 109 us (0.19)
  waiting for transfers between devices: 499 us -> 0 us
  Pallas kernels: 0 us -> 104 us
  matrix products: 37.1 us -> 0 us
  between operations: 15.2 us -> 1.94 us
  local copies, waits for them, and re-layouts: 13.4 us -> 3.29 us
  other arithmetic: 7.13 us -> 0 us
    unnamed x5 -> x0, waiting for transfers between devices: 229 us -> none
    reduce_scatter x2 -> x0, waiting for transfers between devices: 197 us -> none  [the longest x1 145 us: local(): lax.psum_scatter(lax.dot_general(coef, image_unit, (((0,), (0,)), ((), ()...]
    pallas_call x0 -> x1, Pallas kernels: none -> 104 us  [local(): pl.pallas_call(functools.partial(kernel, factor), out_shape=(jax.ShapeDty...]
    all_gather x1 -> x0, waiting for transfers between devices: 73.6 us -> none  [local(): piece = lax.all_gather(text_unit, 'blk', axis=0, tiled=True)]
    dot_general x5 -> x0, matrix products: 37.1 us -> none  [the longest x1 11.9 us: local(): lax.dot_general(coef, image_unit, (((0,), (0,)), ((), ())), preferred_ele...]
    unnamed x13 -> x4, local copies, waits for them, and re-layouts: 13.4 us -> 3.29 us
  transfers between devices with their start and end apart: 4 -> 0, of which waited for: 4 -> 0; matrix products, arithmetic and copies ran while one was open for 3% -> 0% of each run, Pallas kernels for 0% -> 0%
where the time goes in v1:
time: 109 us
  Pallas kernels  104 us (95%)
  local copies, waits for them, and re-layouts  3.29 us (3%)
  between operations  1.94 us (2%)
    pallas_call x1, Pallas kernels, local(): pl.pallas_call(functools.partial(kernel, factor), out_shape=(jax.ShapeDty...  104 us
    unnamed x4, local copies, waits for them, and re-layouts  3.29 us

profile of v1, /device:TPU:1, one launch (start us, length us, event | category | flops | bytes accessed | tf_op | source)
XLA Modules:
  0.0 109.3 jit_solution(13838823909182090758)
XLA Ops:
  1.9 104.0 %shard_map.68 = (f32[256,1536]{1,0:T(8,128)}, f32[96,96]{1,0:T(8,128)}) custom-call(f32[1]{0:T(128)S(6)} %copy.9.lt_ref, f32[1]{0:T(128)S(6)} %copy.10.bias_ref, bf16[256,1536]{1,0:T(8,128)(2,1)} %feats_hbm.1, bf16[1536,1536]{1,0:T(8,128)(2,1)} %hw_hbm.1, bf16[256,1536]{1,0:T(8,128)(2,1)} %text_hbm.1), custom_call_target="tpu_custom_call" | custom-call | flops 20000000000 | bytes 8000000 | tf_op jit(solution)/shard_map/pallas_call | solution.py:493
  106.0 0.0 copy-start
  106.0 2.7 %copy.11 = f32[256,1536]{1,0:T(8,128)} copy(f32[256,1536]{1,0:T(8,128)} %get-tuple-element.4) | data formatting | bytes 3145728
  108.6 0.0 copy-done
  108.6 0.6 copy.12
Async XLA Ops:
  106.0 2.7 %copy-start = (f32[96,96]{1,0:T(8,128)S(1)}, f32[96,96]{1,0:T(8,128)}, u32[]{:S(2)}) copy-start(f32[96,96]{1,0:T(8,128)} %get-tuple-element.5) | copy-start | bytes 110596

commit v2 on v1

v2 whole, which is shorter than its diff:
```python
import functools
import math

import jax
import jax.numpy as jnp
from jax import lax
from jax.experimental import pallas as pl
from jax.experimental.pallas import tpu as pltpu
from jax.sharding import PartitionSpec as P

MESH = pl.DeviceIdType.MESH
F32 = jnp.float32
BF16 = jnp.bfloat16
loss_scale = 4096.0

R = 256
E = 1536
F = 1536
H = 768
NX, NY, NZ = 4, 4, 8
OUT = 96

TEXT_CORE, TEXT_Y, TEXT_FWD = 0, 1, 2
XP1, XM1, XP2, XM2, XP3, XM3 = 3, 4, 5, 6, 7, 8
FT_CORE = 9
U_CORE = 13
CT_CORE = 17
G_CORE = 25
P_Y = 29
Z_RING = 33
Y_SUM = 57
X_SUM = 66
N_SEM = 74

P_CODE = 2.0**33
W_CODE = 2.0**4


def encode(v, s):
    v = v * s
    return (v * v * v).astype(BF16)


def decode(e, s):
    e = e.astype(F32)
    r = jnp.exp2(jnp.log2(jnp.maximum(jnp.abs(e), 1e-37)) * (1.0 / 3.0)) * (1.0 / s)
    return jnp.where(e > 0, r, jnp.where(e < 0, -r, 0.0))


def kernel(
    factor,
    lt_ref, bias_ref, feats_hbm, hw_hbm, text_hbm,
    tgrad_hbm, wgrad_ref,
    hw, ff, ft, u32, inv, uu, txr, tu, sw, pc, cs, cf, pp, yenc, yrecv,
    gg, gs, zs, zr, zfin, zenc, yr2, xenc, xr3, scale_ref,
    load, ss, rs,
):
    dp, blk = lax.axis_index("dp"), lax.axis_index("blk")
    yh, z = dp // NZ, dp % NZ
    yl, x, c = blk // 8, (blk // 2) % NX, blk % 2
    y = yh * 2 + yl

    def dev(x, y, z, c):
        return ((y // 2) * NZ + z, (y % 2) * 8 + x * 2 + c)

    core = dev(x, y, z, 1 - c)
    xp, xm = dev((x + 1) % NX, y, z, c), dev((x + NX - 1) % NX, y, z, c)
    yp = dev(x, yh * 2 + 1 - yl, z, c)
    zp, zm = dev(x, y, (z + 1) % NZ, c), dev(x, y, (z + NZ - 1) % NZ, c)
    ys = [dev(x, (y + k) % NY, z, c) for k in (1, 2, 3)]
    xto = [(2 * c + k // 2, k % 2) for k in range(4)]
    xfrom = x // 2

    loads = [
        pltpu.make_async_copy(text_hbm, txr, load.at[0]),
        pltpu.make_async_copy(feats_hbm, ff.at[pl.ds(0, R)], load.at[1]),
        pltpu.make_async_copy(hw_hbm, hw, load.at[2]),
    ]
    for l in loads:
        l.start()
    bar = pltpu.get_barrier_semaphore()
    for d in [core, xp, xm, zp, zm] + ys:
        pl.semaphore_signal(bar, inc=1, device_id=d, device_id_type=MESH)
    for k in range(NX):
        @pl.when(jnp.logical_not((k == x) & (c == xfrom)))
        def _():
            pl.semaphore_signal(bar, inc=1, device_id=dev(k, y, z, xfrom), device_id_type=MESH)

    scale_ref[...] = jnp.exp(jnp.full((8, 128), lt_ref[0], F32))

    def scale():
        return scale_ref[0:1, 0:1]

    shift = bias_ref[0]

    def norm_text(i, _):
        rows = pl.ds(pl.multiple_of(i * 64, 64), 64)
        t = txr[rows, :].astype(F32)
        ti = lax.rsqrt(jnp.sum(t * t, axis=-1, keepdims=True) + 1e-06)
        tu[pl.ds(pl.multiple_of(c * R + i * 64, 64), 64), :] = (t * ti).astype(BF16)
        return 0

    loads[0].wait()
    lax.fori_loop(0, R // 64, norm_text, 0)

    pl.semaphore_wait(bar, 8 + 4 - jnp.where(c == xfrom, 1, 0))

    sent = []

    def send(src, dst, i, d, j=None):
        cp = pltpu.make_async_remote_copy(
            src, dst, ss.at[i], rs.at[i if j is None else j], device_id=d, device_id_type=MESH
        )
        cp.start()
        sent.append(cp)
        return cp

    trow = pl.ds(pl.multiple_of(c * R, R), R)
    tother = pl.ds(pl.multiple_of(2 * R + c * R, R), R)
    loads[1].wait()
    lo, hi = pl.ds(0, 128), pl.ds(128, 128)

    def half(b, k):
        return pl.ds(b * R + k * 128, 128)

    xp1 = send(ff.at[lo], ff.at[half(1, 0)], XP1, xp)
    xm1 = send(ff.at[hi], ff.at[half(1, 1)], XM1, xm)
    t_y = send(tu.at[trow], tu.at[tother], TEXT_Y, yp)
    t_core = send(tu.at[trow], tu.at[trow], TEXT_CORE, core)
    xp2 = send(ff.at[hi], ff.at[half(2, 0)], XP2, xp)
    xm2 = send(ff.at[lo], ff.at[half(2, 1)], XM2, xm)
    loads[2].wait()

    ft_cp, u_cp, ct_cp, g_cp = {}, {}, {}, {}

    def unit(b):
        rows = pl.ds(b * R, R)
        u32[rows, :] = jnp.dot(ff[rows, :], hw[...], preferred_element_type=F32)

        def norm(i, _):
            r = pl.ds(pl.multiple_of(b * R + i * 64, 64), 64)
            v = u32[r, :]
            iv = lax.rsqrt(jnp.sum(v * v, axis=-1, keepdims=True) + 1e-06)
            v = v * iv
            inv[r, :] = iv
            u32[r, :] = v
            uu[r, :] = v.astype(BF16)
            return 0

        lax.fori_loop(0, 4, norm, 0)
        u_cp[b] = send(uu.at[rows], uu.at[pl.ds(4 * R + b * R, R)], U_CORE + b, core)

        def tr(n, _):
            cols = pl.ds(pl.multiple_of(n * 256, 256), 256)
            ft[cols, pl.ds(b * R, R)] = ff[rows, cols].T
            return 0

        lax.fori_loop(0, 6, tr, 0)
        ft_cp[b] = send(
            ft.at[:, pl.ds(b * R, R)], ft.at[:, pl.ds(4 * R + b * R, R)], FT_CORE + b, core
        )

    def coefs(b, n, h):
        rows = pl.ds(b * R, n * R)
        logits = lax.dot_general(
            uu[rows, :], tu[pl.ds(2 * h * R, 2 * R), :], (((1,), (1,)), ((), ())),
            preferred_element_type=F32,
        )
        p = jax.nn.sigmoid(scale() * logits + shift)
        if h == 0 and b == 0:
            i = lax.broadcasted_iota(jnp.int32, p.shape, 0)
            j = lax.broadcasted_iota(jnp.int32, p.shape, 1)
            p = p - jnp.where(i + c * R == j, 1.0, 0.0)
        p = (factor * p).astype(BF16)
        cf[rows, pl.ds(2 * h * R, 2 * R)] = p
        t0, t1 = p[:, :R].T, p[:, R:].T
        pc[h, :, rows] = jnp.where(c == 0, t0, t1)
        cs[h, :, rows] = jnp.where(c == 0, t1, t0)
        ct_cp[b, h] = send(
            cs.at[h, :, rows], pc.at[h, :, pl.ds(4 * R + b * R, n * R)], CT_CORE + 2 * b + h, core
        )

    def image_grad(b, n):
        rows = pl.ds(b * R, n * R)
        for k in range(2):
            sw[pl.ds(k * H, n * R), :] = jnp.dot(
                cf[rows, :], tu[:, pl.ds(k * H, H)], preferred_element_type=F32
            )

        def chunk(i, _):
            r = pl.ds(pl.multiple_of(b * R + i * 64, 64), 64)
            s = scale()
            g0 = s * sw[pl.ds(pl.multiple_of(i * 64, 64), 64), :]
            g1 = s * sw[pl.ds(pl.multiple_of(H + i * 64, 64), 64), :]
            v0, v1 = u32[r, pl.ds(0, H)], u32[r, pl.ds(H, H)]
            d = jnp.sum(v0 * g0 + v1 * g1, axis=-1, keepdims=True)
            iv = inv[r, :]
            g = [((g0 - v0 * d) * iv).astype(BF16), ((g1 - v1 * d) * iv).astype(BF16)]
            for t in range(3):
                for l in range(2):
                    a0, a1 = g[l][:, t * 128 : t * 128 + 128], g[l][:, 384 + t * 128 : 512 + t * 128]
                    cols = pl.ds((2 * t + l) * 128, 128)
                    gg[r, cols] = jnp.where(c == 0, a0, a1)
                    gs[r, cols] = jnp.where(c == 0, a1, a0)
            return 0

        lax.fori_loop(0, 4 * n, chunk, 0)
        g_cp[b] = send(gs.at[rows], gg.at[pl.ds(4 * R + b * R, n * R)], G_CORE + b, core)

    unit(0)
    t_core.wait_recv()
    coefs(0, 1, 0)
    xp1.wait_recv()
    xp3 = send(ff.at[half(1, 0)], ff.at[half(3, 0)], XP3, xp)
    xm1.wait_recv()
    xm3 = send(ff.at[half(1, 1)], ff.at[half(3, 1)], XM3, xm)
    unit(1)
    coefs(1, 1, 0)
    t_y.wait_recv()
    t_fwd = send(tu.at[tother], tu.at[tother], TEXT_FWD, core)
    xp2.wait_recv()
    xm2.wait_recv()
    unit(2)
    coefs(2, 1, 0)
    t_fwd.wait_recv()
    coefs(0, 3, 1)
    image_grad(0, 3)
    xp3.wait_recv()
    xm3.wait_recv()
    unit(3)
    coefs(3, 1, 0)
    coefs(3, 1, 1)
    image_grad(3, 1)
    for b in range(4):
        ft_cp[b].wait_recv()
    g_cp[0].wait_recv()
    g_cp[3].wait_recv()

    def weight(n):
        cols = pl.ds(n * 256, 256)
        sw[:, cols] = jnp.dot(ft[...], gg[:, cols], preferred_element_type=F32)

    def own(n, zz, k):
        return sw[pl.ds(pl.multiple_of(k * H + zz * OUT, 32), OUT), pl.ds(n * 256, 256)]

    ring = {}

    def step(n, s):
        cps = []
        for d in range(2):
            zz = (z + (4 - s if d == 0 else NZ - 4 + s)) % NZ
            i = (n * 2 + d) * 4 + s
            if s:
                ring[n, s - 1][d].wait_recv()
            for k in range(2):
                if s == 0 and k != d:
                    continue
                v = own(n, zz, k)
                if s > 1 or (s == 1 and k == d):
                    v = v + decode(zr[i - 1, pl.ds(k * OUT, OUT), :], W_CODE)
                zs[i, pl.ds(k * OUT, OUT), :] = encode(v, W_CODE)
            r = pl.ds(d * OUT, OUT) if s == 0 else pl.ds(0, 2 * OUT)
            cps.append(send(zs.at[i, r], zr.at[i, r], Z_RING + i, zp if d == 0 else zm))
        ring[n, s] = cps

    y_cp = {}

    def final(n):
        for d in range(2):
            ring[n, 3][d].wait_recv()
        cols = pl.ds(n * 256, 256)
        for k in range(2):
            r = pl.ds(k * OUT, OUT)
            v = own(n, z, k)
            for d in range(2):
                v = v + decode(zr[(n * 2 + d) * 4 + 3, r, :], W_CODE)
            zfin[r, cols] = v
            zenc[r, cols] = encode(v, W_CODE)
        for k in range(3):
            r, cc = yslice(n, (y + k + 1) % NY)
            y_cp[n, k] = send(zenc.at[r, cc], yr2.at[n, k], Y_SUM + 3 * n + k, ys[k])

    def yslice(n, yy):
        return (
            pl.ds(pl.multiple_of((yy // 2) * OUT, 32), OUT),
            pl.ds(pl.multiple_of(n * 256 + (yy % 2) * 128, 128), 128),
        )

    x_cp = []

    def over_x(n):
        r, cc = yslice(n, y)
        v = zfin[r, cc]
        for k in range(3):
            y_cp[n, k].wait_recv()
            v = v + decode(yr2[n, k], W_CODE)
        xenc[n] = encode(v, W_CODE)
        for k in range(4):
            j = n - k // 2
            if j not in (0, 1):
                continue
            xx, kc = xto[k]
            cols = pl.ds(j * 128, 128)
            cp = pltpu.make_async_remote_copy(
                xenc.at[n], xr3.at[x, :, cols], ss.at[X_SUM + len(x_cp)], rs.at[X_SUM + 4 * j + x],
                device_id=dev(xx, y, z, kc), device_id_type=MESH,
            )
            mine = (xx == x) & (kc == c)

            @pl.when(jnp.logical_not(mine))
            def _():
                cp.start()

            @pl.when(mine)
            def _():
                xr3[x, :, cols] = xenc[n]

            x_cp.append((cp, mine))

    out_cp = []

    def text_side(h):
        pp[h] = jnp.dot(pc[h], uu[...], preferred_element_type=F32)

    p_cp = []

    def text_send():
        for i in range(4):
            r = pl.ds(i * 64, 64)
            yenc[r, :] = encode(pp[1, r, :], P_CODE)
            p_cp.append(send(yenc.at[r], yrecv.at[r], P_Y + i, yp))

    def text_out(i):
        p_cp[i].wait_recv()
        r = pl.ds(i * 64, 64)
        t = txr[r, :].astype(F32)
        ti = lax.rsqrt(jnp.sum(t * t, axis=-1, keepdims=True) + 1e-06)
        t = t * ti
        g = scale() * (pp[0, r, :] + decode(yrecv[r, :], P_CODE))
        pp[0, r, :] = (g - t * jnp.sum(t * g, axis=-1, keepdims=True)) * ti
        cp = pltpu.make_async_copy(pp.at[0, r], tgrad_hbm.at[r], load.at[3 + i])
        cp.start()
        out_cp.append(cp)

    weight(0)
    step(0, 0)
    weight(1)
    step(1, 0)
    step(0, 1)
    weight(2)
    step(2, 0)
    step(1, 1)
    for b in range(4):
        u_cp[b].wait_recv()
    for key in ct_cp:
        ct_cp[key].wait_recv()
    text_side(1)
    text_send()
    step(2, 1)
    step(0, 2)
    text_side(0)
    step(1, 2)
    step(2, 2)
    step(0, 3)
    step(1, 3)
    step(2, 3)
    text_out(0)
    final(0)
    text_out(1)
    final(1)
    text_out(2)
    over_x(0)
    final(2)
    text_out(3)
    over_x(1)
    over_x(2)

    for j in range(2):
        for k in range(4):
            @pl.when(jnp.logical_not((k == x) & (c == xfrom)))
            def _():
                pltpu.make_async_remote_copy(
                    xenc.at[0], xr3.at[k, :, pl.ds(j * 128, 128)],
                    ss.at[X_SUM + 4 * j + k], rs.at[X_SUM + 4 * j + k],
                    device_id=core, device_id_type=MESH,
                ).wait_recv()

    v = decode(xr3[0], W_CODE)
    for k in range(1, 4):
        v = v + decode(xr3[k], W_CODE)
    mine = 2 * (x % 2) + c
    out = v[:, :OUT]
    for k, off in ((1, 96), (2, 64), (3, 160)):
        out = jnp.where(mine == k, pltpu.roll(v, 256 - off, 1)[:, :OUT], out)
    wgrad_ref[...] = out

    for cp in sent:
        cp.wait_send()
    for cp, mine in x_cp:
        @pl.when(jnp.logical_not(mine))
        def _():
            cp.wait_send()
    for cp in out_cp:
        cp.wait()


def local(feats, head_weight, text_raw, log_temp, bias):
    rows = feats.shape[0]
    factor = loss_scale / (lax.axis_size("dp") * rows * lax.axis_size("blk"))
    vmem = pltpu.VMEM
    scratch = [
        vmem((F, E), BF16),
        vmem((4 * R, F), BF16),
        vmem((F, 8 * R), BF16),
        vmem((4 * R, E), F32),
        vmem((4 * R, 1), F32),
        vmem((8 * R, E), BF16),
        vmem((R, E), BF16),
        vmem((4 * R, E), BF16),
        vmem((F, H), F32),
        vmem((2, R, 8 * R), BF16),
        vmem((2, R, 4 * R), BF16),
        vmem((4 * R, 4 * R), BF16),
        vmem((2, R, E), F32),
        vmem((R, E), BF16),
        vmem((R, E), BF16),
        vmem((8 * R, H), BF16),
        vmem((4 * R, H), BF16),
        vmem((24, 2 * OUT, 256), BF16),
        vmem((24, 2 * OUT, 256), BF16),
        vmem((2 * OUT, H), F32),
        vmem((2 * OUT, H), BF16),
        vmem((3, 3, OUT, 128), BF16),
        vmem((3, OUT, 128), BF16),
        vmem((4, OUT, 256), BF16),
        vmem((8, 128), F32),
        pltpu.SemaphoreType.DMA((7,)),
        pltpu.SemaphoreType.DMA((N_SEM,)),
        pltpu.SemaphoreType.DMA((N_SEM,)),
    ]
    anyspec = pl.BlockSpec(memory_space=pl.ANY)
    smem = pl.BlockSpec(memory_space=pltpu.SMEM)
    return pl.pallas_call(
        functools.partial(kernel, factor),
        out_shape=(
            jax.ShapeDtypeStruct((R, E), F32),
            jax.ShapeDtypeStruct((OUT, OUT), F32),
        ),
        in_specs=[smem, smem, anyspec, anyspec, anyspec],
        out_specs=(anyspec, pl.BlockSpec(memory_space=pltpu.VMEM)),
        scratch_shapes=scratch,
        compiler_params=pltpu.CompilerParams(
            collective_id=0, has_side_effects=True, vmem_limit_bytes=63 * 1024 * 1024
        ),
        cost_estimate=pl.CostEstimate(
            flops=20_000_000_000, bytes_accessed=8_000_000, transcendentals=4_000_000
        ),
    )(log_temp, bias, feats, head_weight, text_raw)


def solution(mesh):
    return jax.shard_map(
        local,
        mesh=mesh,
        in_specs=(P(("dp", "blk"), None), P(), P(("dp", "blk"), None), P(), P()),
        out_specs=(P(("dp", "blk"), None), P("dp", "blk")),
        check_vma=False,
    )
```

time: 109 us -> 95.6 us (0.88); the launches traced: 109 us -> 94.6 us
  Pallas kernels: 104 us -> 89.3 us
    pallas_call x1, Pallas kernels: 104 us -> 89.3 us  [local(): pl.pallas_call(functools.partial(kernel, factor), out_shape=(jax.ShapeDty...]
where the time goes in v2:
time: 95.6 us; the launch traced here: 94.6 us
  Pallas kernels  89.3 us (93%)
  local copies, waits for them, and re-layouts  3.29 us (3%)
  between operations  1.94 us (2%)
    pallas_call x1, Pallas kernels, local(): pl.pallas_call(functools.partial(kernel, factor), out_shape=(jax.ShapeDty...  89.3 us
    unnamed x4, local copies, waits for them, and re-layouts  3.29 us

profile of v2, /device:TPU:1, one launch (start us, length us, event | category | flops | bytes accessed | tf_op | source)
XLA Modules:
  0.0 94.6 jit_solution(5151274565152309422)
XLA Ops:
  1.9 89.3 %shard_map.68 = (f32[256,1536]{1,0:T(8,128)}, f32[96,96]{1,0:T(8,128)}) custom-call(f32[1]{0:T(128)S(6)} %copy.9.lt_ref, f32[1]{0:T(128)S(6)} %copy.10.bias_ref, bf16[256,1536]{1,0:T(8,128)(2,1)} %feats_hbm.1, bf16[1536,1536]{1,0:T(8,128)(2,1)} %hw_hbm.1, bf16[256,1536]{1,0:T(8,128)(2,1)} %text_hbm.1), custom_call_target="tpu_custom_call" | custom-call | flops 20000000000 | bytes 8000000 | tf_op jit(solution)/shard_map/pallas_call | solution.py:443
  91.3 0.0 copy-start
  91.3 2.7 %copy.11 = f32[256,1536]{1,0:T(8,128)} copy(f32[256,1536]{1,0:T(8,128)} %get-tuple-element.4) | data formatting | bytes 3145728
  94.0 0.0 copy-done
  94.0 0.6 copy.12
Async XLA Ops:
  91.3 2.7 %copy-start = (f32[96,96]{1,0:T(8,128)S(1)}, f32[96,96]{1,0:T(8,128)}, u32[]{:S(2)}) copy-start(f32[96,96]{1,0:T(8,128)} %get-tuple-element.5) | copy-start | bytes 110596

commit v3 on v2

--- a/solution.py
+++ b/solution.py
@@ -100,9 +100,6 @@
         tu[pl.ds(pl.multiple_of(c * R + i * 64, 64), 64), :] = (t * ti).astype(BF16)
         return 0
 
-    loads[0].wait()
-    lax.fori_loop(0, R // 64, norm_text, 0)
-
     pl.semaphore_wait(bar, 8 + 4 - jnp.where(c == xfrom, 1, 0))
 
     sent = []
@@ -125,76 +122,81 @@
 
     xp1 = send(ff.at[lo], ff.at[half(1, 0)], XP1, xp)
     xm1 = send(ff.at[hi], ff.at[half(1, 1)], XM1, xm)
+    xp2 = send(ff.at[hi], ff.at[half(2, 0)], XP2, xp)
+    xm2 = send(ff.at[lo], ff.at[half(2, 1)], XM2, xm)
+    loads[0].wait()
+    lax.fori_loop(0, R // 64, norm_text, 0)
     t_y = send(tu.at[trow], tu.at[tother], TEXT_Y, yp)
     t_core = send(tu.at[trow], tu.at[trow], TEXT_CORE, core)
-    xp2 = send(ff.at[hi], ff.at[half(2, 0)], XP2, xp)
-    xm2 = send(ff.at[lo], ff.at[half(2, 1)], XM2, xm)
     loads[2].wait()
 
     ft_cp, u_cp, ct_cp, g_cp = {}, {}, {}, {}
+
+    alone = pl.when(dp >= 0)
 
     def unit(b):
         rows = pl.ds(b * R, R)
-        u32[rows, :] = jnp.dot(ff[rows, :], hw[...], preferred_element_type=F32)
+
+        @alone
+        def _():
+            u32[rows, :] = jnp.dot(ff[rows, :], hw[...], preferred_element_type=F32)
+            ft[:, rows] = ff[rows, :].T
 
         def norm(i, _):
             r = pl.ds(pl.multiple_of(b * R + i * 64, 64), 64)
             v = u32[r, :]
             iv = lax.rsqrt(jnp.sum(v * v, axis=-1, keepdims=True) + 1e-06)
-            v = v * iv
             inv[r, :] = iv
-            u32[r, :] = v
-            uu[r, :] = v.astype(BF16)
+            uu[r, :] = (v * iv).astype(BF16)
             return 0
 
         lax.fori_loop(0, 4, norm, 0)
         u_cp[b] = send(uu.at[rows], uu.at[pl.ds(4 * R + b * R, R)], U_CORE + b, core)
-
-        def tr(n, _):
-            cols = pl.ds(pl.multiple_of(n * 256, 256), 256)
-            ft[cols, pl.ds(b * R, R)] = ff[rows, cols].T
-            return 0
-
-        lax.fori_loop(0, 6, tr, 0)
         ft_cp[b] = send(
-            ft.at[:, pl.ds(b * R, R)], ft.at[:, pl.ds(4 * R + b * R, R)], FT_CORE + b, core
+            ft.at[:, rows], ft.at[:, pl.ds(4 * R + b * R, R)], FT_CORE + b, core
         )
 
     def coefs(b, n, h):
         rows = pl.ds(b * R, n * R)
-        logits = lax.dot_general(
-            uu[rows, :], tu[pl.ds(2 * h * R, 2 * R), :], (((1,), (1,)), ((), ())),
-            preferred_element_type=F32,
-        )
-        p = jax.nn.sigmoid(scale() * logits + shift)
-        if h == 0 and b == 0:
-            i = lax.broadcasted_iota(jnp.int32, p.shape, 0)
-            j = lax.broadcasted_iota(jnp.int32, p.shape, 1)
-            p = p - jnp.where(i + c * R == j, 1.0, 0.0)
-        p = (factor * p).astype(BF16)
-        cf[rows, pl.ds(2 * h * R, 2 * R)] = p
-        t0, t1 = p[:, :R].T, p[:, R:].T
-        pc[h, :, rows] = jnp.where(c == 0, t0, t1)
-        cs[h, :, rows] = jnp.where(c == 0, t1, t0)
+
+        @alone
+        def _():
+            logits = lax.dot_general(
+                uu[rows, :], tu[pl.ds(2 * h * R, 2 * R), :], (((1,), (1,)), ((), ())),
+                preferred_element_type=F32,
+            )
+            p = jax.nn.sigmoid(scale() * logits + shift)
+            if h == 0 and b == 0:
+                i = lax.broadcasted_iota(jnp.int32, p.shape, 0)
+                j = lax.broadcasted_iota(jnp.int32, p.shape, 1)
+                p = p - jnp.where(i + c * R == j, 1.0, 0.0)
+            p = (factor * p).astype(BF16)
+            cf[rows, pl.ds(2 * h * R, 2 * R)] = p
+            t0, t1 = p[:, :R].T, p[:, R:].T
+            pc[h, :, rows] = jnp.where(c == 0, t0, t1)
+            cs[h, :, rows] = jnp.where(c == 0, t1, t0)
+
         ct_cp[b, h] = send(
             cs.at[h, :, rows], pc.at[h, :, pl.ds(4 * R + b * R, n * R)], CT_CORE + 2 * b + h, core
         )
 
     def image_grad(b, n):
         rows = pl.ds(b * R, n * R)
-        for k in range(2):
-            sw[pl.ds(k * H, n * R), :] = jnp.dot(
-                cf[rows, :], tu[:, pl.ds(k * H, H)], preferred_element_type=F32
-            )
+
+        @alone
+        def _():
+            for k in range(2):
+                sw[pl.ds(k * H, n * R), :] = jnp.dot(
+                    cf[rows, :], tu[:, pl.ds(k * H, H)], preferred_element_type=F32
+                )
 
         def chunk(i, _):
             r = pl.ds(pl.multiple_of(b * R + i * 64, 64), 64)
-            s = scale()
-            g0 = s * sw[pl.ds(pl.multiple_of(i * 64, 64), 64), :]
-            g1 = s * sw[pl.ds(pl.multiple_of(H + i * 64, 64), 64), :]
-            v0, v1 = u32[r, pl.ds(0, H)], u32[r, pl.ds(H, H)]
+            iv = inv[r, :]
+            g0 = sw[pl.ds(pl.multiple_of(i * 64, 64), 64), :]
+            g1 = sw[pl.ds(pl.multiple_of(H + i * 64, 64), 64), :]
+            v0, v1 = u32[r, pl.ds(0, H)] * iv, u32[r, pl.ds(H, H)] * iv
             d = jnp.sum(v0 * g0 + v1 * g1, axis=-1, keepdims=True)
-            iv = inv[r, :]
             g = [((g0 - v0 * d) * iv).astype(BF16), ((g1 - v1 * d) * iv).astype(BF16)]
             for t in range(3):
                 for l in range(2):
@@ -238,7 +240,10 @@
 
     def weight(n):
         cols = pl.ds(n * 256, 256)
-        sw[:, cols] = jnp.dot(ft[...], gg[:, cols], preferred_element_type=F32)
+
+        @alone
+        def _():
+            sw[:, cols] = jnp.dot(ft[...], gg[:, cols], preferred_element_type=F32)
 
     def own(n, zz, k):
         return sw[pl.ds(pl.multiple_of(k * H + zz * OUT, 32), OUT), pl.ds(n * 256, 256)]
@@ -319,8 +324,12 @@
 
     out_cp = []
 
-    def text_side(h):
-        pp[h] = jnp.dot(pc[h], uu[...], preferred_element_type=F32)
+    def text_side(h, k):
+        cols = pl.ds(k * H, H)
+
+        @alone
+        def _():
+            pp[h, :, cols] = jnp.dot(pc[h], uu[:, cols], preferred_element_type=F32)
 
     p_cp = []
 
@@ -333,11 +342,15 @@
     def text_out(i):
         p_cp[i].wait_recv()
         r = pl.ds(i * 64, 64)
-        t = txr[r, :].astype(F32)
-        ti = lax.rsqrt(jnp.sum(t * t, axis=-1, keepdims=True) + 1e-06)
-        t = t * ti
-        g = scale() * (pp[0, r, :] + decode(yrecv[r, :], P_CODE))
-        pp[0, r, :] = (g - t * jnp.sum(t * g, axis=-1, keepdims=True)) * ti
+
+        @alone
+        def _():
+            t = txr[r, :].astype(F32)
+            ti = lax.rsqrt(jnp.sum(t * t, axis=-1, keepdims=True) + 1e-06)
+            t = t * ti
+            g = pp[0, r, :] + decode(yrecv[r, :], P_CODE)
+            pp[0, r, :] = (g - t * jnp.sum(t * g, axis=-1, keepdims=True)) * ti
+
         cp = pltpu.make_async_copy(pp.at[0, r], tgrad_hbm.at[r], load.at[3 + i])
         cp.start()
         out_cp.append(cp)
@@ -346,29 +359,31 @@
     step(0, 0)
     weight(1)
     step(1, 0)
-    step(0, 1)
     weight(2)
     step(2, 0)
-    step(1, 1)
     for b in range(4):
         u_cp[b].wait_recv()
     for key in ct_cp:
         ct_cp[key].wait_recv()
-    text_side(1)
+    step(0, 1)
+    text_side(1, 0)
+    step(1, 1)
+    text_side(1, 1)
     text_send()
     step(2, 1)
     step(0, 2)
-    text_side(0)
+    text_side(0, 0)
+    text_side(0, 1)
     step(1, 2)
     step(2, 2)
+    text_out(0)
     step(0, 3)
     step(1, 3)
+    text_out(1)
     step(2, 3)
-    text_out(0)
+    text_out(2)
     final(0)
-    text_out(1)
     final(1)
-    text_out(2)
     over_x(0)
     final(2)
     text_out(3)
@@ -440,7 +455,7 @@
     ]
     anyspec = pl.BlockSpec(memory_space=pl.ANY)
     smem = pl.BlockSpec(memory_space=pltpu.SMEM)
-    return pl.pallas_call(
+    text_grad, weight_grad = pl.pallas_call(
         functools.partial(kernel, factor),
         out_shape=(
             jax.ShapeDtypeStruct((R, E), F32),
@@ -456,6 +471,8 @@
             flops=20_000_000_000, bytes_accessed=8_000_000, transcendentals=4_000_000
         ),
     )(log_temp, bias, feats, head_weight, text_raw)
+    scale = jnp.exp(log_temp[0])
+    return scale * text_grad, scale * weight_grad
 
 
 def solution(mesh):

time: 95.6 us -> 88.6 us (0.927)
  Pallas kernels: 89.3 us -> 82.5 us
  other arithmetic: 0 us -> 3.29 us
  local copies, waits for them, and re-layouts: 3.29 us -> 0.01 us
    pallas_call x1, Pallas kernels: 89.3 us -> 82.5 us  [local(): pl.pallas_call(functools.partial(kernel, factor), out_shape=(jax.ShapeDty...]
    mul x0 -> x2, other arithmetic: none -> 3.29 us  [local(): return (scale * text_grad, scale * weight_grad)]
    unnamed x4 -> x2, local copies, waits for them, and re-layouts: 3.29 us -> 0.01 us
where the time goes in v3:
time: 88.6 us; the launch traced here: 87.8 us
  Pallas kernels  82.5 us (93%)
  other arithmetic  3.29 us (4%)
  between operations  1.98 us (2%)
    pallas_call x1, Pallas kernels, local(): pl.pallas_call(functools.partial(kernel, factor), out_shape=(jax.ShapeDty...  82.5 us
    mul x2, other arithmetic, local(): return (scale * text_grad, scale * weight_grad)  3.29 us

profile of v3, /device:TPU:1, one launch (start us, length us, event | category | flops | bytes accessed | tf_op | source)
XLA Modules:
  0.0 87.8 jit_solution(2667285822895309396)
XLA Ops:
  2.0 82.5 %shard_map.68 = (f32[256,1536]{1,0:T(8,128)}, f32[96,96]{1,0:T(8,128)}) custom-call(f32[1]{0:T(128)S(6)} %copy.7.lt_ref, f32[1]{0:T(128)S(6)} %copy.8.bias_ref, bf16[256,1536]{1,0:T(8,128)(2,1)} %feats_hbm.1, bf16[1536,1536]{1,0:T(8,128)(2,1)} %hw_hbm.1, bf16[256,1536]{1,0:T(8,128)(2,1)} %text_hbm.1), custom_call_target="tpu_custom_call" | custom-call | flops 20000000000 | bytes 8000000 | tf_op jit(solution)/shard_map/pallas_call | solution.py:458
  84.5 0.0 copy-start
  84.5 2.7 %broadcast_multiply_fusion = f32[256,1536]{1,0:T(8,128)} fusion(f32[256,1536]{1,0:T(8,128)} %get-tuple-element.4, f32[]{:T(128)} %bitcast), kind=kLoop, calls=%fused_computation | loop fusion | flops 393216 | bytes 3145732 | tf_op jit(solution)/shard_map/mul | solution.py:475
  87.1 0.0 copy-done
  87.2 0.6 broadcast_multiply_fusion.1
Async XLA Ops:
  84.5 2.7 %copy-start = (f32[96,96]{1,0:T(8,128)S(1)}, f32[96,96]{1,0:T(8,128)}, u32[]{:S(2)}) copy-start(f32[96,96]{1,0:T(8,128)} %get-tuple-element.5) | copy-start | bytes 110596

commit v4 on v3

--- a/solution.py
+++ b/solution.py
@@ -28,9 +28,9 @@
 G_CORE = 25
 P_Y = 29
 Z_RING = 33
-Y_SUM = 57
-X_SUM = 66
-N_SEM = 74
+Y_SUM = 81
+X_SUM = 90
+N_SEM = 98
 
 P_CODE = 2.0**33
 W_CODE = 2.0**4
@@ -50,7 +50,7 @@
 def kernel(
     factor,
     lt_ref, bias_ref, feats_hbm, hw_hbm, text_hbm,
-    tgrad_hbm, wgrad_ref,
+    tgrad_ref, wgrad_ref,
     hw, ff, ft, u32, inv, uu, txr, tu, sw, pc, cs, cf, pp, yenc, yrecv,
     gg, gs, zs, zr, zfin, zenc, yr2, xenc, xr3, scale_ref,
     load, ss, rs,
@@ -250,29 +250,32 @@
 
     ring = {}
 
+    def hop(n, d, k, s):
+        zz = (z + (4 - s if d == 0 else NZ - 4 + s)) % NZ
+        i = (n * 2 + d) * 4 + s
+        r = pl.ds(k * OUT, OUT)
+        v = own(n, zz, k)
+        if s > (0 if k == d else 1):
+            ring[n, d, k, s - 1].wait_recv()
+            v = v + decode(zr[i - 1, r, :], W_CODE)
+        zs[i, r, :] = encode(v, W_CODE)
+        ring[n, d, k, s] = send(
+            zs.at[i, r], zr.at[i, r], Z_RING + 2 * i + k, zp if d == 0 else zm
+        )
+
     def step(n, s):
-        cps = []
         for d in range(2):
-            zz = (z + (4 - s if d == 0 else NZ - 4 + s)) % NZ
-            i = (n * 2 + d) * 4 + s
-            if s:
-                ring[n, s - 1][d].wait_recv()
-            for k in range(2):
-                if s == 0 and k != d:
-                    continue
-                v = own(n, zz, k)
-                if s > 1 or (s == 1 and k == d):
-                    v = v + decode(zr[i - 1, pl.ds(k * OUT, OUT), :], W_CODE)
-                zs[i, pl.ds(k * OUT, OUT), :] = encode(v, W_CODE)
-            r = pl.ds(d * OUT, OUT) if s == 0 else pl.ds(0, 2 * OUT)
-            cps.append(send(zs.at[i, r], zr.at[i, r], Z_RING + i, zp if d == 0 else zm))
-        ring[n, s] = cps
+            hop(n, d, d, s)
+        if s < 3:
+            for d in range(2):
+                hop(n, d, 1 - d, s + 1)
 
     y_cp = {}
 
     def final(n):
         for d in range(2):
-            ring[n, 3][d].wait_recv()
+            for k in range(2):
+                ring[n, d, k, 3].wait_recv()
         cols = pl.ds(n * 256, 256)
         for k in range(2):
             r = pl.ds(k * OUT, OUT)
@@ -322,7 +325,6 @@
 
             x_cp.append((cp, mine))
 
-    out_cp = []
 
     def text_side(h, k):
         cols = pl.ds(k * H, H)
@@ -349,44 +351,40 @@
             ti = lax.rsqrt(jnp.sum(t * t, axis=-1, keepdims=True) + 1e-06)
             t = t * ti
             g = pp[0, r, :] + decode(yrecv[r, :], P_CODE)
-            pp[0, r, :] = (g - t * jnp.sum(t * g, axis=-1, keepdims=True)) * ti
-
-        cp = pltpu.make_async_copy(pp.at[0, r], tgrad_hbm.at[r], load.at[3 + i])
-        cp.start()
-        out_cp.append(cp)
+            tgrad_ref[r, :] = (g - t * jnp.sum(t * g, axis=-1, keepdims=True)) * ti
 
     weight(0)
     step(0, 0)
     weight(1)
     step(1, 0)
-    weight(2)
-    step(2, 0)
     for b in range(4):
         u_cp[b].wait_recv()
     for key in ct_cp:
         ct_cp[key].wait_recv()
-    step(0, 1)
     text_side(1, 0)
-    step(1, 1)
     text_side(1, 1)
     text_send()
+    step(0, 1)
+    weight(2)
+    step(2, 0)
+    step(1, 1)
+    step(0, 2)
     step(2, 1)
-    step(0, 2)
     text_side(0, 0)
+    step(1, 2)
     text_side(0, 1)
-    step(1, 2)
+    step(0, 3)
     step(2, 2)
     text_out(0)
-    step(0, 3)
     step(1, 3)
     text_out(1)
+    final(0)
     step(2, 3)
     text_out(2)
-    final(0)
     final(1)
     over_x(0)
+    text_out(3)
     final(2)
-    text_out(3)
     over_x(1)
     over_x(2)
 
@@ -415,8 +413,6 @@
         @pl.when(jnp.logical_not(mine))
         def _():
             cp.wait_send()
-    for cp in out_cp:
-        cp.wait()
 
 
 def local(feats, head_weight, text_raw, log_temp, bias):
@@ -449,7 +445,7 @@
         vmem((3, OUT, 128), BF16),
         vmem((4, OUT, 256), BF16),
         vmem((8, 128), F32),
-        pltpu.SemaphoreType.DMA((7,)),
+        pltpu.SemaphoreType.DMA((3,)),
         pltpu.SemaphoreType.DMA((N_SEM,)),
         pltpu.SemaphoreType.DMA((N_SEM,)),
     ]
@@ -458,14 +454,14 @@
     text_grad, weight_grad = pl.pallas_call(
         functools.partial(kernel, factor),
         out_shape=(
-            jax.ShapeDtypeStruct((R, E), F32),
+            pltpu.VMEM((R, E), F32),
             jax.ShapeDtypeStruct((OUT, OUT), F32),
         ),
         in_specs=[smem, smem, anyspec, anyspec, anyspec],
-        out_specs=(anyspec, pl.BlockSpec(memory_space=pltpu.VMEM)),
+        out_specs=(pl.BlockSpec(memory_space=pltpu.VMEM), pl.BlockSpec(memory_space=pltpu.VMEM)),
         scratch_shapes=scratch,
         compiler_params=pltpu.CompilerParams(
-            collective_id=0, has_side_effects=True, vmem_limit_bytes=63 * 1024 * 1024
+            collective_id=0, has_side_effects=True, vmem_limit_bytes=59 * 1024 * 1024
         ),
         cost_estimate=pl.CostEstimate(
             flops=20_000_000_000, bytes_accessed=8_000_000, transcendentals=4_000_000

time: 88.6 us -> 86.3 us (0.974)
  other arithmetic: 3.29 us -> 1.88 us
    mul x2, other arithmetic: 3.29 us -> 1.88 us  [local(): return (scale * text_grad, scale * weight_grad)]
where the time goes in v4:
time: 86.3 us; the launch traced here: 86.2 us
  Pallas kernels  82.4 us (95%)
  between operations  1.98 us (2%)
  other arithmetic  1.88 us (2%)
    pallas_call x1, Pallas kernels, local(): pl.pallas_call(functools.partial(kernel, factor), out_shape=(pltpu.VMEM((...  82.4 us
    mul x2, other arithmetic, local(): return (scale * text_grad, scale * weight_grad)  1.88 us

profile of v4, /device:TPU:1, one launch (start us, length us, event | category | flops | bytes accessed | tf_op | source)
XLA Modules:
  0.0 86.2 jit_solution(11432195278893107926)
XLA Ops:
  2.0 82.4 %shard_map.68 = (f32[256,1536]{1,0:T(8,128)S(1)}, f32[96,96]{1,0:T(8,128)}) custom-call(f32[1]{0:T(128)S(6)} %copy.7.lt_ref, f32[1]{0:T(128)S(6)} %copy.8.bias_ref, bf16[256,1536]{1,0:T(8,128)(2,1)} %feats_hbm.1, bf16[1536,1536]{1,0:T(8,128)(2,1)} %hw_hbm.1, bf16[256,1536]{1,0:T(8,128)(2,1)} %text_hbm.1), custom_call_target="tpu_custom_call" | custom-call | flops 20000000000 | bytes 8000000 | tf_op jit(solution)/shard_map/pallas_call | solution.py:454
  84.3 0.0 copy-start
  84.3 1.3 %broadcast_multiply_fusion = f32[256,1536]{1,0:T(8,128)} fusion(f32[256,1536]{1,0:T(8,128)S(1)} %get-tuple-element.4, f32[]{:T(128)} %bitcast), kind=kLoop, calls=%fused_computation | loop fusion | flops 393216 | bytes 3145732 | tf_op jit(solution)/shard_map/mul | solution.py:471
  85.6 0.0 copy-done
  85.6 0.6 broadcast_multiply_fusion.1
Async XLA Ops:
  84.3 1.3 %copy-start = (f32[96,96]{1,0:T(8,128)S(1)}, f32[96,96]{1,0:T(8,128)}, u32[]{:S(2)}) copy-start(f32[96,96]{1,0:T(8,128)} %get-tuple-element.5) | copy-start | bytes 110596

commit v5 on v4

--- a/solution.py
+++ b/solution.py
@@ -377,15 +377,15 @@
     step(2, 2)
     text_out(0)
     step(1, 3)
+    final(0)
     text_out(1)
-    final(0)
     step(2, 3)
-    text_out(2)
     final(1)
     over_x(0)
+    final(2)
+    text_out(2)
+    over_x(1)
     text_out(3)
-    final(2)
-    over_x(1)
     over_x(2)
 
     for j in range(2):

time: 86.3 us -> 86.5 us (level)
  no operation moved by 1% of the time
where the time goes in v5:
time: 86.5 us; the launch traced here: 86.4 us
  Pallas kernels  82.5 us (95%)
  between operations  1.98 us (2%)
  other arithmetic  1.88 us (2%)
    pallas_call x1, Pallas kernels, local(): pl.pallas_call(functools.partial(kernel, factor), out_shape=(pltpu.VMEM((...  82.5 us
    mul x2, other arithmetic, local(): return (scale * text_grad, scale * weight_grad)  1.88 us

profile of v5, /device:TPU:1, one launch (start us, length us, event | category | flops | bytes accessed | tf_op | source)
XLA Modules:
  0.0 86.4 jit_solution(8237073525236796575)
XLA Ops:
  2.0 82.5 %shard_map.68 = (f32[256,1536]{1,0:T(8,128)S(1)}, f32[96,96]{1,0:T(8,128)}) custom-call(f32[1]{0:T(128)S(6)} %copy.7.lt_ref, f32[1]{0:T(128)S(6)} %copy.8.bias_ref, bf16[256,1536]{1,0:T(8,128)(2,1)} %feats_hbm.1, bf16[1536,1536]{1,0:T(8,128)(2,1)} %hw_hbm.1, bf16[256,1536]{1,0:T(8,128)(2,1)} %text_hbm.1), custom_call_target="tpu_custom_call" | custom-call | flops 20000000000 | bytes 8000000 | tf_op jit(solution)/shard_map/pallas_call | solution.py:454
  84.5 0.0 copy-start
  84.5 1.3 %broadcast_multiply_fusion = f32[256,1536]{1,0:T(8,128)} fusion(f32[256,1536]{1,0:T(8,128)S(1)} %get-tuple-element.4, f32[]{:T(128)} %bitcast), kind=kLoop, calls=%fused_computation | loop fusion | flops 393216 | bytes 3145732 | tf_op jit(solution)/shard_map/mul | solution.py:471
  85.8 0.0 copy-done
  85.8 0.6 broadcast_multiply_fusion.1
Async XLA Ops:
  84.5 1.3 %copy-start = (f32[96,96]{1,0:T(8,128)S(1)}, f32[96,96]{1,0:T(8,128)}, u32[]{:S(2)}) copy-start(f32[96,96]{1,0:T(8,128)} %get-tuple-element.5) | copy-start | bytes 110596

commit v6 on v4

--- a/solution.py
+++ b/solution.py
@@ -277,13 +277,17 @@
             for k in range(2):
                 ring[n, d, k, 3].wait_recv()
         cols = pl.ds(n * 256, 256)
-        for k in range(2):
-            r = pl.ds(k * OUT, OUT)
-            v = own(n, z, k)
-            for d in range(2):
-                v = v + decode(zr[(n * 2 + d) * 4 + 3, r, :], W_CODE)
-            zfin[r, cols] = v
-            zenc[r, cols] = encode(v, W_CODE)
+
+        @alone
+        def _():
+            for k in range(2):
+                r = pl.ds(k * OUT, OUT)
+                v = own(n, z, k)
+                for d in range(2):
+                    v = v + decode(zr[(n * 2 + d) * 4 + 3, r, :], W_CODE)
+                zfin[r, cols] = v
+                zenc[r, cols] = encode(v, W_CODE)
+
         for k in range(3):
             r, cc = yslice(n, (y + k + 1) % NY)
             y_cp[n, k] = send(zenc.at[r, cc], yr2.at[n, k], Y_SUM + 3 * n + k, ys[k])
@@ -338,7 +342,11 @@
     def text_send():
         for i in range(4):
             r = pl.ds(i * 64, 64)
-            yenc[r, :] = encode(pp[1, r, :], P_CODE)
+
+            @alone
+            def _():
+                yenc[r, :] = encode(pp[1, r, :], P_CODE)
+
             p_cp.append(send(yenc.at[r], yrecv.at[r], P_Y + i, yp))
 
     def text_out(i):

time: 86.3 us -> 86.3 us (level)
  no operation moved by 1% of the time
where the time goes in v6:
time: 86.3 us; the launch traced here: 86.2 us
  Pallas kernels  82.4 us (95%)
  between operations  1.98 us (2%)
  other arithmetic  1.88 us (2%)
    pallas_call x1, Pallas kernels, local(): pl.pallas_call(functools.partial(kernel, factor), out_shape=(pltpu.VMEM((...  82.4 us
    mul x2, other arithmetic, local(): return (scale * text_grad, scale * weight_grad)  1.88 us

profile of v6, /device:TPU:1, one launch (start us, length us, event | category | flops | bytes accessed | tf_op | source)
XLA Modules:
  0.0 86.2 jit_solution(5222915230583651235)
XLA Ops:
  2.0 82.4 %shard_map.68 = (f32[256,1536]{1,0:T(8,128)S(1)}, f32[96,96]{1,0:T(8,128)}) custom-call(f32[1]{0:T(128)S(6)} %copy.7.lt_ref, f32[1]{0:T(128)S(6)} %copy.8.bias_ref, bf16[256,1536]{1,0:T(8,128)(2,1)} %feats_hbm.1, bf16[1536,1536]{1,0:T(8,128)(2,1)} %hw_hbm.1, bf16[256,1536]{1,0:T(8,128)(2,1)} %text_hbm.1), custom_call_target="tpu_custom_call" | custom-call | flops 20000000000 | bytes 8000000 | tf_op jit(solution)/shard_map/pallas_call | solution.py:462
  84.4 0.0 copy-start
  84.4 1.3 %broadcast_multiply_fusion = f32[256,1536]{1,0:T(8,128)} fusion(f32[256,1536]{1,0:T(8,128)S(1)} %get-tuple-element.4, f32[]{:T(128)} %bitcast), kind=kLoop, calls=%fused_computation | loop fusion | flops 393216 | bytes 3145732 | tf_op jit(solution)/shard_map/mul | solution.py:479
  85.6 0.0 copy-done
  85.6 0.6 broadcast_multiply_fusion.1
Async XLA Ops:
  84.4 1.3 %copy-start = (f32[96,96]{1,0:T(8,128)S(1)}, f32[96,96]{1,0:T(8,128)}, u32[]{:S(2)}) copy-start(f32[96,96]{1,0:T(8,128)} %get-tuple-element.5) | copy-start | bytes 110596
